TPU v7x, 32 devices: a whole 2x2x4 slice. The times are simulated.
32 devices in a mesh: grp: 2 (over y), section: 2 (over core), seq: 4 (over z), fsdp: 2 (over x).
Axes of the slice: x: 2, y: 2, z: 4, core: 2. Of those that a mesh axis runs over, the one named last changes fastest.
Arguments:
- head_inputs: bfloat16 [2, 4, 256, 7680], P('section', ('grp', 'fsdp'), 'seq'), parts along dimension 1, may hold values from -8 to 8
- hidden: bfloat16 [2, 4, 256, 2560], P('section', ('grp', 'fsdp'), 'seq'), parts along dimension 1, may hold values from -3 to 3
- out_weight: bfloat16 [2, 2560, 2560], P('section', 'fsdp'), may hold values from -0.125 to 0.125
- time_weight: bfloat16 [2, 256, 7680], P('section', None, ('seq', 'fsdp')), may hold values from -0.375 to 0.375
- head_weight: bfloat16 [2, 2560, 64], P('section', ('seq', 'fsdp')), may hold values from -0.125 to 0.125
- latent: float32 [2, 4, 128, 128], P('section', ('grp', 'fsdp'), 'seq'), parts along dimension 1, may hold values from -6 to 6
- timesteps: int32 [2, 4, 2], P('section', ('grp', 'fsdp')), parts along dimension 1, may hold values from 41 to 999, as said below
Outputs:
- velocity: float32 [2, 4, 128, 128], P('section', ('grp', 'fsdp'), 'seq'), parts along dimension 1
- carried: float32 [2, 4, 128, 128], P('section', ('grp', 'fsdp'), 'seq'), parts along dimension 1
There are 2 independent parts, one for each index of `grp`. A program takes and returns all parts, laid end to end along the dimension named above; an argument that names none is the same for every part. Nothing has to cross between parts.
Inputs may be any that keep to these rules, and one draw needn't show every extreme that they name: timesteps[0] lie in 875 to 999 and timesteps[1] in 100 to 874 for the current entry; the next entry is the current one minus 10 to 59.
All inputs are finite; a program needn't handle non-finite values.
Results may differ from a plain program's by a relative error of at most 0.0049.
Values may be sent and summed in bfloat16 or wider, within the bound.
A program may use at most 128 MiB of HBM per device.

v0:
```python
import math

import jax
import jax.numpy as jnp
from jax import lax
from jax.sharding import PartitionSpec as P

DIM = 2560
HEADS = 32
HEAD = 80
PATCH = 64
FREQ = 256


def partner(block, axis, apart):
    count = lax.axis_size(axis)
    route = []
    for low in range(count):
        high = low | 1 << apart
        if high != low and high < count:
            route += [(low, high), (high, low)]
    return lax.ppermute(block, axis, route)


def time_embed(steps_now):
    half = FREQ // 2
    freqs = jnp.exp(-math.log(10000.0) * jnp.arange(half, dtype=jnp.float32) / half)
    angle = steps_now.astype(jnp.float32)[..., None] * freqs
    return jnp.concatenate([jnp.cos(angle), jnp.sin(angle)], axis=-1)


def sigma_of(steps_now):
    unit_time = steps_now.astype(jnp.float32) / 1000.0
    return 5.0 * unit_time / (1.0 + 4.0 * unit_time)


def attend(exchanged):
    items = exchanged.shape[0]
    length = exchanged.shape[1]
    local_heads = exchanged.shape[2]
    query_all = exchanged[..., :HEAD]
    key_rows = exchanged[..., HEAD : 2 * HEAD]
    value_rows = exchanged[..., 2 * HEAD :]
    block_rows = min(512, length)
    block_count = length // block_rows

    def one_block(block_index):
        query_block = lax.dynamic_slice_in_dim(query_all, block_index * block_rows, block_rows, 1)
        scores = jnp.einsum(
            "nqhe,nkhe->nhqk", query_block, key_rows, preferred_element_type=jnp.float32
        ) * HEAD ** (-0.5)
        row_max = jnp.max(scores, axis=-1, keepdims=True)
        exp_scores = jnp.exp(scores - row_max)
        row_sum = jnp.sum(exp_scores, axis=-1, keepdims=True)
        weights = (exp_scores / row_sum).astype(jnp.bfloat16)
        return jnp.einsum(
            "nhqk,nkhe->nqhe", weights, value_rows, preferred_element_type=jnp.float32
        ).astype(jnp.bfloat16)

    blocks = lax.map(one_block, jnp.arange(block_count, dtype=jnp.int32))
    return blocks.transpose(1, 0, 2, 3, 4).reshape(items, length, local_heads * HEAD)


def body(head_inputs, hidden, out_weight, time_weight, head_weight, latent, timesteps):
    samples = head_inputs.shape[1]
    row_count = head_inputs.shape[2]
    flat_count = samples * row_count
    local = head_inputs.reshape(samples, row_count, HEADS, 3 * HEAD)
    attended = lax.all_to_all(
        attend(lax.all_to_all(local, "seq", split_axis=2, concat_axis=1, tiled=True)),
        "seq",
        split_axis=1,
        concat_axis=2,
        tiled=True,
    )
    flattened = attended.reshape(flat_count, HEADS * HEAD)
    time_full, head_full = (
        lax.all_gather(time_weight, ("seq", "fsdp"), axis=2, tiled=True),
        lax.all_gather(head_weight, ("seq", "fsdp"), axis=1, tiled=True),
    )
    embedding = time_embed(timesteps[0, :, 0]).astype(jnp.bfloat16)
    modulation = jnp.dot(embedding, time_full[0], preferred_element_type=jnp.float32)
    gate_term = modulation[:, None, :DIM]
    shift_term = modulation[:, None, DIM : 2 * DIM]
    scale_term = modulation[:, None, 2 * DIM :]
    own_columns = lax.all_to_all(flattened, "fsdp", split_axis=1, concat_axis=0, tiled=True)
    projected = lax.psum_scatter(
        jnp.dot(own_columns, out_weight[0], preferred_element_type=jnp.float32).astype(
            jnp.bfloat16
        ),
        "fsdp",
        scatter_dimension=0,
        tiled=True,
    ).astype(jnp.float32)
    updated = hidden.reshape(samples, row_count, DIM).astype(
        jnp.float32
    ) + gate_term * projected.reshape(samples, row_count, DIM)
    average = jnp.mean(updated, axis=-1, keepdims=True)
    centred = updated - average
    variance = jnp.mean(centred * centred, axis=-1, keepdims=True)
    normed = (centred * lax.rsqrt(variance + 1e-06) * (1.0 + scale_term) + shift_term).astype(
        jnp.bfloat16
    )
    velocity = jnp.dot(
        normed.reshape(flat_count, DIM), head_full[0], preferred_element_type=jnp.float32
    )
    velocity = velocity.reshape(1, samples, row_count // 2, 2 * PATCH)
    step_size = sigma_of(timesteps[0, :, 1]) - sigma_of(timesteps[0, :, 0])
    stepped = latent + step_size[None, :, None, None] * velocity
    carried = partner(stepped, "section", 0)
    return (velocity, carried)


def solution(mesh):
    return jax.shard_map(
        body,
        mesh=mesh,
        in_specs=(
            P("section", ("grp", "fsdp"), "seq", None),
            P("section", ("grp", "fsdp"), "seq", None),
            P("section", "fsdp", None),
            P("section", None, ("seq", "fsdp")),
            P("section", ("seq", "fsdp"), None),
            P("section", ("grp", "fsdp"), "seq", None),
            P("section", ("grp", "fsdp"), None),
        ),
        out_specs=(
            P("section", ("grp", "fsdp"), "seq", None),
            P("section", ("grp", "fsdp"), "seq", None),
        ),
        check_vma=False,
    )
```

profile of v0, /device:TPU:0, one launch (start us, length us, event | category | flops | bytes accessed | tf_op | source)
XLA Modules:
  0.0 164.6 jit_solution(13938546322388415020)
XLA Ops:
  8.0 0.0 all-gather.2.cloned.1.call-start
  8.0 0.7 all-gather.2.cloned.1.call-update
  8.7 0.0 reduce-scatter.2.cloned.1.call-start
  8.8 3.5 %reshape.152 = bf16[1,64,32,240]{3,2,1,0:T(8,128)(2,1)S(1)} reshape(bf16[1,1,64,7680]{3,2,1,0:T(8,128)(2,1)} %param.7) | data formatting | bytes 1966080 | tf_op jit(solution)/shard_map/reshape | solution.py:68
  12.3 0.6 copy.28
  12.9 47.6 %all_to_all.52 = bf16[1,64,32,240]{3,1,0,2:T(8,128)(2,1)S(1)} all-to-all(bf16[1,64,32,240]{3,1,0,2:T(8,128)(2,1)S(1)} %copy.28), channel_id=1, replica_groups=mesh['grp'=2,'section'=2,'seq'=4,'fsdp'=2] {'seq'}, dimensions={2} | all-to-all | bytes 1966080 | tf_op jit(solution)/shard_map/all_to_all | solution.py:70
  60.6 0.6 copy.46
  61.1 0.1 copy.30
  61.2 0.4 fusion.35
  61.6 0.3 copy.42
  62.0 0.3 copy.43
  62.3 0.3 copy.44
  62.6 2.2 %fusion.37 = (f32[8,256]{1,0:T(8,128)S(1)}, f32[8,256,256]{1,2,0:T(8,128)}) fusion(bf16[1,256,8,80]{1,3,2,0:T(8,128)(2,1)S(1)} %copy.44, bf16[1,256,8,80]{1,3,2,0:T(8,128)(2,1)S(1)} %copy.43), kind=kOutput, calls=%fused_computation.41 | convolution fusion | flops 85459200 | bytes 2760704 | tf_op jit(solution)/shard_map/while/body/eval_jaxpr/sub | solution.py:53
  64.8 1.9 %convolution_convert_fusion = bf16[8,256,80]{1,2,0:T(8,128)(2,1)S(1)} fusion(f32[8,256,256]{1,2,0:T(8,128)} %get-tuple-element.26, f32[8,256]{1,0:T(8,128)S(1)} %get-tuple-element.25, bf16[1,256,8,80]{1,3,2,0:T(8,128)(2,1)S(1)} %copy.42), kind=kOutput, calls=%fused_computation.10 | convolution fusion | flops 85098496 | bytes 2760704 | tf_op jit(solution)/shard_map/while/body/eval_jaxpr/nhqk,nkhe->nqhe/dot_general | solution.py:56
  66.7 0.6 copy.35
  67.3 0.5 broadcast.88
  67.8 2.6 %reduce.14 = bf16[256,640]{1,0:T(8,128)(2,1)S(1)} reduce(bf16[256,1,640]{2,1,0:T(2,128)(2,1)S(1)} %bitcast.71, bf16[]{:T(256)} %broadcast.88), dimensions={1}, to_apply=%bitcast.60.reduce_sub_computation | reduce | bytes 655362
  70.4 0.1 reshape.166
  70.5 22.7 %all_to_all.53 = bf16[4,2,20480]{2,1,0:T(2,128)(2,1)S(1)} all-to-all(bf16[4,2,20480]{2,1,0:T(2,128)(2,1)S(1)} %reshape.166), channel_id=1, replica_groups=mesh['grp'=2,'section'=2,'seq'=4,'fsdp'=2] {'seq'}, dimensions={0} | all-to-all | bytes 655360 | tf_op jit(solution)/shard_map/all_to_all | solution.py:69
  93.3 0.3 reshape.167
  93.6 0.3 copy.36
  93.9 0.2 all_to_all.45
  94.2 8.1 %all_to_all.54 = bf16[64,2,1280]{2,0,1:T(8,128)(2,1)S(1)} all-to-all(bf16[64,2,1280]{2,0,1:T(8,128)(2,1)S(1)} %copy.37), channel_id=1, replica_groups=mesh['grp'=2,'section'=2,'seq'=4,'fsdp'=2] {'fsdp'}, dimensions={1} | all-to-all | bytes 655360 | tf_op jit(solution)/shard_map/all_to_all | solution.py:86
  102.3 0.0 copy-start.4
  102.3 0.0 copy-start.2
  102.3 4.7 %fusion.5 = bf16[128,2560]{1,0:T(8,128)(2,1)} fusion(bf16[128,1280]{1,0:T(8,128)(2,1)S(1)} %bitcast.73, bf16[1,1280,2560]{2,1,0:T(8,128)(2,1)} %param.9), kind=kOutput, calls=%fused_computation.5 | convolution fusion | flops 839188480 | bytes 7536640 | tf_op jit(solution)/shard_map/dot_general | solution.py:88
  107.0 0.0 reduce-scatter.2.cloned.1.call-update
  107.0 0.0 copy-done.4
  107.0 0.6 fusion.36
  108.9 0.1 sine_convert_fusion
  109.0 0.0 copy-done.2
  109.0 0.2 copy.38
  109.2 38.0 %all_gather.7 = bf16[1,2560,64]{2,0,1:T(2,128)(2,1)S(1)} all-gather(bf16[1,320,64]{2,0,1:T(2,128)(2,1)S(1)} %copy.38), channel_id=1, replica_groups=mesh['grp'=2,'section'=2,'seq'=4,'fsdp'=2] {'seq','fsdp'}, dimensions={1}, use_global_device_ids=true | all-gather | bytes 368640 | tf_op jit(solution)/shard_map/all_gather | solution.py:79
  147.2 0.8 copy.39
  148.0 0.0 copy-start
  148.1 0.0 all-gather.2.cloned.1.call-done
  148.1 3.2 %fusion.3 = f32[1,7680]{1,0:T(1,128)S(1)} fusion(bf16[256,1]{0,1:T(2,128)(2,1)S(1)} %reshape.160, bf16[1,256,7680]{1,2,0:T(8,128)(2,1)} %all-gather.2.cloned.1.call-done), kind=kOutput, calls=%fused_computation.3 | convolution fusion | flops 3932160 | bytes 3963392 | tf_op jit(solution)/shard_map/dot_general | solution.py:82
  151.3 0.0 copy-start.3
  151.3 0.1 slice_reduce_fusion.1
  151.4 0.0 reduce-scatter.2.cloned.1.call-done
  151.5 0.0 copy-done
  151.5 1.2 fusion.10
  152.7 1.2 multiply_reduce_fusion.1
  153.9 1.3 fusion.11
  155.2 0.1 reshape.156
  155.3 0.0 copy-start.1
  155.3 0.0 copy-done.3
  155.3 0.1 collective-permute-start
  155.4 1.2 collective-permute-done
  156.6 0.6 copy.48
  157.2 0.0 copy-done.1
  (7 shorter events, 0.1 us)
Async XLA Ops:
  8.0 140.1 %all-gather.2.cloned.1.call-start = ((), (), s32[]{:S(2)}) async-start(), calls=%async_computation.4 | async-start | bytes 4423680 | tf_op jit(solution)/shard_map/all_gather | solution.py:78
  8.7 142.7 %reduce-scatter.2.cloned.1.call-start = ((), (), s32[]{:S(2)}) async-start(), calls=%async_computation.5 | async-start | bytes 983040 | tf_op jit(solution)/shard_map/reduce_scatter | solution.py:87
  102.3 4.8 %copy-start.4 = (s32[1,1,2]{2,1,0:T(1,128)S(1)}, s32[1,1,2]{2,1,0:T(1,128)}, u32[]{:S(2)}) copy-start(s32[1,1,2]{2,1,0:T(1,128)} %param.13) | copy-start | bytes 28
  102.3 6.7 %copy-start.2 = (bf16[1,320,64]{1,2,0:T(8,128)(2,1)S(1)}, bf16[1,320,64]{1,2,0:T(8,128)(2,1)}, u32[]{:S(2)}) copy-start(bf16[1,320,64]{1,2,0:T(8,128)(2,1)} %param.11) | copy-start | bytes 122884
  148.0 3.5 %copy-start = (bf16[1,1,64,2560]{3,2,1,0:T(8,128)(2,1)S(1)}, bf16[1,1,64,2560]{3,2,1,0:T(8,128)(2,1)}, u32[]{:S(2)}) copy-start(bf16[1,1,64,2560]{3,2,1,0:T(8,128)(2,1)} %param.8) | copy-start | bytes 983044
  151.3 4.0 %copy-start.3 = (f32[1,1,32,128]{3,2,1,0:T(8,128)S(1)}, f32[1,1,32,128]{3,2,1,0:T(8,128)}, u32[]{:S(2)}) copy-start(f32[1,1,32,128]{3,2,1,0:T(8,128)} %param.12) | copy-start | bytes 49156
  155.3 1.9 %copy-start.1 = (f32[1,1,32,128]{3,2,1,0:T(8,128)}, f32[1,1,32,128]{3,2,1,0:T(8,128)S(1)}, u32[]{:S(2)}) copy-start(f32[1,1,32,128]{3,2,1,0:T(8,128)S(1)} %reshape.156) | copy-start | bytes 49156
  155.3 1.2 collective-permute-start
Sparse Core Ops, SparseCore 0:
  11.3 94.5 all-gather.1
Sparse Core Ops, SparseCore 1:
  107.1 27.4 reduce-scatter.1
where the time goes:
time: 165 us
  blocking collectives  116 us (70%)
  between operations  17.1 us (10%)
  matrix products  13.4 us (8%)
  local copies, waits for them, and re-layouts  10.4 us (6%)
  other arithmetic  5.18 us (3%)
  waiting for transfers between devices  1.92 us (1%)
    all_to_all x1, blocking collectives, body(): lax.all_to_all(local, 'seq', split_axis=2, concat_axis=1, tiled=True)  47.6 us
    all_gather x1, blocking collectives, body(): lax.all_gather(head_weight, ('seq', 'fsdp'), axis=1, tiled=True)  38 us
    all_to_all x1, blocking collectives, body(): lax.all_to_all(attend(lax.all_to_all(local, 'seq', split_axis=2, concat_a...  22.7 us
    all_to_all x1, blocking collectives, body(): lax.all_to_all(flattened, 'fsdp', split_axis=1, concat_axis=0, tiled=True)  8.11 us
    dot_general x1, matrix products, body(): jnp.dot(own_columns, out_weight[0], preferred_element_type=jnp.float32)  4.74 us
    reshape x2, local copies, waits for them, and re-layouts, body(): local = head_inputs.reshape(samples, row_count, HEADS, 3 * HEAD)  4.12 us
  transfers between devices with their start and end apart: 3, of which 1 were waited for; matrix products, arithmetic and copies ran while one was open for 15% of the time, Pallas kernels for 0%

commit v1 on v0

--- a/solution.py
+++ b/solution.py
@@ -1,8 +1,12 @@
+import functools
 import math
 
 import jax
 import jax.numpy as jnp
+import numpy as np
 from jax import lax
+from jax.experimental import pallas as pl
+from jax.experimental.pallas import tpu as pltpu
 from jax.sharding import PartitionSpec as P
 
 DIM = 2560
@@ -111,9 +115,376 @@
     return (velocity, carried)
 
 
+MESH = pl.DeviceIdType.MESH
+BF16 = jnp.bfloat16
+F32 = jnp.float32
+
+
+def up(value, step):
+    return -(-value // step) * step
+
+
+class Plan:
+    def __init__(self, seq, fsdp, rows):
+        self.seq, self.fsdp, self.rows = seq, fsdp, rows
+        self.heads = HEADS // seq
+        self.group_in = self.heads * 3 * HEAD
+        self.group_out = self.heads * HEAD
+        per = max(1, self.heads // 4)
+        self.chunks = []
+        lo_in = lo_out = 0
+        for first in range(0, self.heads, per):
+            last = min(first + per, self.heads)
+            hi_in = min(up(last * 3 * HEAD, 128), self.group_in)
+            hi_out = last * HEAD // 128 * 128 if last < self.heads else self.group_out
+            self.chunks.append((first, last, (lo_in, hi_in), (lo_out, hi_out)))
+            lo_in, lo_out = hi_in, hi_out
+        self.block = 512
+        self.blocks = DIM // self.block
+
+
+def fused(
+    plan, qkv, hid, ow, tw, hw, lat, ts, freqs, vel_out, car_out,
+    qkv_v, ow_v, tw_v, hw_v, hid_v, lat_v, emb, mod_loc, mod_all, att, gath, own, part, got, packed, head_v,
+    upd, vel_v, step_v, step_in,
+    loc_sem, own_sem, qs, qr, es, er, ms, mr, hxs, hxr, hzs, hzr, as_, ar, ps, pr, cs, cr,
+):
+    seq, fsdp, rows = plan.seq, plan.fsdp, plan.rows
+    z, f, s = lax.axis_index("seq"), lax.axis_index("fsdp"), lax.axis_index("section")
+    other = 1 - f
+    slot = z * fsdp + f
+    per_half = seq // fsdp
+    n_chunks = len(plan.chunks)
+
+    def remote(src, dst, send, recv, to):
+        return pltpu.make_async_remote_copy(
+            src_ref=src, dst_ref=dst, send_sem=send, recv_sem=recv, device_id=to, device_id_type=MESH
+        )
+
+    barrier = pltpu.get_barrier_semaphore()
+    for dz in range(seq):
+        for df in range(fsdp):
+            if dz or df:
+                to = {"seq": z ^ dz, "fsdp": f ^ df}
+                pl.semaphore_signal(barrier, inc=1, device_id=to, device_id_type=MESH)
+    pl.semaphore_signal(barrier, inc=1, device_id={"section": 1 - s}, device_id_type=MESH)
+
+    loads = [
+        pltpu.make_async_copy(hw.at[0], hw_v, loc_sem.at[0]),
+        pltpu.make_async_copy(tw.at[0], tw_v, loc_sem.at[1]),
+        pltpu.make_async_copy(ow.at[0], ow_v, loc_sem.at[2]),
+        pltpu.make_async_copy(hid.at[0, 0], hid_v, loc_sem.at[3]),
+        pltpu.make_async_copy(lat.at[0, 0], lat_v, loc_sem.at[4]),
+    ]
+
+    def group_of(position):
+        return lax.rem(position, fsdp) * per_half + position // fsdp
+
+    def columns(position, span):
+        first = group_of(position) * plan.group_in + span[0]
+        return pl.ds(pl.multiple_of(first, 128), span[1] - span[0])
+
+    def my_rows(position):
+        return pl.ds(pl.multiple_of(position * rows, rows), rows)
+
+    own_loads = []
+    for c, (_, _, span, _) in enumerate(plan.chunks):
+        own_loads.append(
+            pltpu.make_async_copy(
+                qkv.at[0, 0, :, columns(z, span)],
+                qkv_v.at[my_rows(z), span[0] : span[1]],
+                own_sem.at[c],
+            )
+        )
+        own_loads[-1].start()
+    for load in loads:
+        load.start()
+
+    t_now = ts[0, 0, 0].astype(F32)
+    angle = t_now * jnp.broadcast_to(freqs[...], (8, FREQ // 2))
+    emb[f, :, : FREQ // 2] = jnp.cos(angle)
+    emb[f, :, FREQ // 2 :] = jnp.sin(angle)
+
+    pl.semaphore_wait(barrier, seq * fsdp)
+
+    order = sorted(range(1, seq), reverse=True)
+    sends = []
+    emb_copy = remote(emb.at[f], emb.at[f], es, er, {"fsdp": other})
+    emb_copy.start()
+    in_copies = []
+    for c, (_, _, span, _) in enumerate(plan.chunks):
+        row = []
+        for d in order:
+            peer = z ^ d
+            row.append(
+                remote(
+                    qkv.at[0, 0, :, columns(peer, span)],
+                    qkv_v.at[my_rows(z), span[0] : span[1]],
+                    qs.at[c, d],
+                    qr.at[c, d],
+                    {"seq": peer},
+                )
+            )
+            row[-1].start()
+        in_copies.append(row)
+
+    loads[0].wait()
+    half_rows = hw_v.shape[0] // 2
+    packed[slot] = jnp.concatenate([hw_v[:half_rows], hw_v[half_rows:]], axis=1)
+    head_copy = remote(packed.at[slot], packed.at[slot], hxs, hxr, {"fsdp": other})
+    head_copy.start()
+
+    emb_copy.wait()
+    loads[1].wait()
+    both = emb[...].reshape(fsdp * 8, FREQ).astype(BF16)
+    mod = jnp.dot(both, tw_v[...], preferred_element_type=F32)
+    for b in range(fsdp):
+        mod_loc[b] = mod[b * 8 : b * 8 + 1]
+    mod_all[slot] = mod_loc[f]
+    mod_copies = []
+    for dz in range(seq):
+        for df in range(fsdp):
+            if dz or df:
+                mod_copies.append(
+                    remote(
+                        mod_loc.at[f ^ df],
+                        mod_all.at[slot],
+                        ms.at[dz, df],
+                        mr.at[dz, df],
+                        {"seq": z ^ dz, "fsdp": f ^ df},
+                    )
+                )
+                mod_copies[-1].start()
+
+    half = lax.rem(z, fsdp)
+    part_of_half = z // fsdp
+    for c, (first, last, _, span) in enumerate(plan.chunks):
+        own_loads[c].wait()
+        for copy in in_copies[c]:
+            copy.wait_recv()
+        for h in range(first, last):
+            base = h * 3 * HEAD
+            query = qkv_v[:, base : base + HEAD]
+            key = qkv_v[:, base + HEAD : base + 2 * HEAD]
+            value = qkv_v[:, base + 2 * HEAD : base + 3 * HEAD]
+            scores = lax.dot_general(
+                query, key, (((1,), (1,)), ((), ())), preferred_element_type=F32
+            ) * HEAD ** (-0.5)
+            exps = jnp.exp(scores - jnp.max(scores, axis=-1, keepdims=True))
+            weights = (exps * (1.0 / jnp.sum(exps, axis=-1, keepdims=True))).astype(BF16)
+            att[:, h * HEAD : (h + 1) * HEAD] = jnp.dot(
+                weights, value, preferred_element_type=F32
+            ).astype(BF16)
+        lo, hi = span
+        for d in [*order, 0]:
+            peer = z ^ d
+            source = att.at[my_rows(peer), lo:hi]
+            target = gath.at[f, part_of_half, :, lo:hi]
+            if d:
+                remote(
+                    source, target, as_.at[c, d], ar.at[c, f, part_of_half], {"seq": peer, "fsdp": half}
+                ).start()
+            else:
+
+                @pl.when(half == f)
+                def _():
+                    pltpu.make_async_copy(source, target, ar.at[c, f, part_of_half]).start()
+
+                @pl.when(half != f)
+                def _():
+                    remote(
+                        source, target, as_.at[c, d], ar.at[c, f, part_of_half], {"fsdp": half}
+                    ).start()
+
+    head_copy.wait()
+    head_copies = []
+    for d in order:
+        for b, index in enumerate((slot, z * fsdp + other)):
+            head_copies.append(
+                remote(packed.at[index], packed.at[index], hzs.at[b, d], hzr.at[b, d], {"seq": z ^ d})
+            )
+            head_copies[-1].start()
+
+    loads[2].wait()
+    for c, (_, _, _, (lo, hi)) in enumerate(plan.chunks):
+        for b in range(fsdp):
+            for i in range(per_half):
+                block = gath.at[b, i, :, lo:hi]
+                pltpu.make_async_copy(block, block, ar.at[c, b, i]).wait()
+    part_copies = []
+    for k in range(plan.blocks):
+        cols = slice(k * plan.block, (k + 1) * plan.block)
+        total = jnp.zeros((fsdp * rows, plan.block), F32)
+        for i in range(per_half):
+            total += jnp.dot(
+                gath[:, i].reshape(fsdp * rows, plan.group_out),
+                ow_v[i * plan.group_out : (i + 1) * plan.group_out, cols],
+                preferred_element_type=F32,
+            )
+        for b in range(fsdp):
+            own[b, :, cols] = total[b * rows : (b + 1) * rows]
+            part[b, :, cols] = total[b * rows : (b + 1) * rows].astype(BF16)
+        part_copies.append(
+            remote(part.at[other, :, cols], got.at[:, cols], ps.at[k], pr.at[k], {"fsdp": other})
+        )
+        part_copies[-1].start()
+
+    for copy in head_copies:
+        copy.wait_recv()
+    for j in range(seq * fsdp):
+        block = packed[j]
+        swapped = jnp.concatenate([block[:, PATCH:], block[:, :PATCH]], axis=1)
+        left = lax.broadcasted_iota(jnp.int32, block.shape, 1) < PATCH
+        head_v[2 * half_rows * j : 2 * half_rows * j + half_rows] = jnp.where(left, block, swapped)
+        head_v[2 * half_rows * j + half_rows : 2 * half_rows * (j + 1)] = jnp.where(
+            left, swapped, block
+        )
+    for copy in mod_copies:
+        copy.wait_recv()
+    modulation = jnp.concatenate([mod_all[j] for j in range(seq * fsdp)], axis=1)
+    gate = modulation[:, :DIM]
+    shift = modulation[:, DIM : 2 * DIM]
+    scale = modulation[:, 2 * DIM :]
+    loads[3].wait()
+    loads[4].wait()
+
+    sums = jnp.zeros((rows, 1), F32)
+    for k in range(plan.blocks):
+        cols = slice(k * plan.block, (k + 1) * plan.block)
+        part_copies[k].wait_recv()
+        projected = own[f, :, cols] + got[:, cols].astype(F32)
+        now = hid_v[:, cols].astype(F32) + gate[:, cols] * projected
+        upd[:, cols] = now
+        sums += jnp.sum(now, axis=-1, keepdims=True)
+    centred = upd[...] - sums * (1.0 / DIM)
+    variance = jnp.mean(centred * centred, axis=-1, keepdims=True)
+    normed = (centred * lax.rsqrt(variance + 1e-06) * (1.0 + scale) + shift).astype(BF16)
+    vel_v[...] = jnp.dot(normed, head_v[...], preferred_element_type=F32)
+    even = vel_v[pl.ds(0, rows // 2, 2), :]
+    odd = vel_v[pl.ds(1, rows // 2, 2), :]
+    left = lax.broadcasted_iota(jnp.int32, even.shape, 1) < PATCH
+    velocity = jnp.where(left, even, odd)
+    vel_out[0, 0] = velocity
+
+    unit = jnp.full((1, 2 * PATCH), ts[0, 0, 0].astype(F32), F32) / 1000.0
+    unit_next = jnp.full((1, 2 * PATCH), ts[0, 0, 1].astype(F32), F32) / 1000.0
+    step = 5.0 * unit_next / (1.0 + 4.0 * unit_next) - 5.0 * unit / (1.0 + 4.0 * unit)
+    step_v[...] = lat_v[...] + step * velocity
+    swap = remote(step_v, step_in, cs, cr, {"section": 1 - s})
+    swap.start()
+
+    for row in in_copies:
+        for copy in row:
+            copy.wait_send()
+    for copy in mod_copies + head_copies + part_copies:
+        copy.wait_send()
+    for c, (_, _, _, (lo, hi)) in enumerate(plan.chunks):
+        for d in order:
+            block = att.at[0:rows, lo:hi]
+            pltpu.make_async_copy(block, block, as_.at[c, d]).wait()
+
+        @pl.when(half != f)
+        def _():
+            block = att.at[0:rows, lo:hi]
+            pltpu.make_async_copy(block, block, as_.at[c, 0]).wait()
+
+    swap.wait()
+    car_out[0, 0] = step_in[...]
+
+
+def fused_body(plan, head_inputs, hidden, out_weight, time_weight, head_weight, latent, timesteps):
+    seq, fsdp, rows = plan.seq, plan.fsdp, plan.rows
+    chunks = len(plan.chunks)
+    per_half = seq // fsdp
+    half = FREQ // 2
+    freqs = np.exp(-math.log(10000.0) * np.arange(half) / half).astype(np.float32)[None]
+    dma = pltpu.SemaphoreType.DMA
+    vmem = pltpu.VMEM
+    whole = pl.BlockSpec(memory_space=pltpu.VMEM)
+    anywhere = pl.BlockSpec(memory_space=pl.ANY)
+    parts = seq * fsdp
+    return pl.pallas_call(
+        functools.partial(fused, plan),
+        out_shape=(
+            jax.ShapeDtypeStruct(latent.shape, F32),
+            jax.ShapeDtypeStruct(latent.shape, F32),
+        ),
+        in_specs=[anywhere] * 6 + [pl.BlockSpec(memory_space=pltpu.SMEM), whole],
+        out_specs=(whole, whole),
+        scratch_shapes=[
+            vmem((seq * rows, plan.group_in), BF16),
+            vmem(out_weight.shape[1:], BF16),
+            vmem(time_weight.shape[1:], BF16),
+            vmem(head_weight.shape[1:], BF16),
+            vmem((rows, DIM), BF16),
+            vmem(latent.shape[2:], F32),
+            vmem((fsdp, 8, FREQ), F32),
+            vmem((fsdp, 1, time_weight.shape[2]), F32),
+            vmem((parts, 1, time_weight.shape[2]), F32),
+            vmem((seq * rows, plan.group_out), BF16),
+            vmem((fsdp, per_half, rows, plan.group_out), BF16),
+            vmem((fsdp, rows, DIM), F32),
+            vmem((fsdp, rows, DIM), BF16),
+            vmem((rows, DIM), BF16),
+            vmem((parts, head_weight.shape[1] // 2, 2 * PATCH), BF16),
+            vmem((DIM, 2 * PATCH), BF16),
+            vmem((rows, DIM), F32),
+            vmem((rows, 2 * PATCH), F32),
+            vmem(latent.shape[2:], F32),
+            vmem(latent.shape[2:], F32),
+            dma((5,)),
+            dma((chunks,)),
+            dma((chunks, seq)),
+            dma((chunks, seq)),
+            dma,
+            dma,
+            dma((seq, fsdp)),
+            dma((seq, fsdp)),
+            dma,
+            dma,
+            dma((fsdp, seq)),
+            dma((fsdp, seq)),
+            dma((chunks, seq)),
+            dma((chunks, fsdp, per_half)),
+            dma((plan.blocks,)),
+            dma((plan.blocks,)),
+            dma,
+            dma,
+        ],
+        compiler_params=pltpu.CompilerParams(
+            collective_id=0, has_side_effects=True, vmem_limit_bytes=40 * 2**20
+        ),
+        name="fused_step",
+    )(head_inputs, hidden, out_weight, time_weight, head_weight, latent, timesteps, freqs)
+
+
+def pick(mesh):
+    seq, fsdp, sections = mesh.shape["seq"], mesh.shape["fsdp"], mesh.shape["section"]
+
+    def run(*blocks):
+        samples, rows = blocks[0].shape[1:3]
+        fits = (
+            samples == 1
+            and fsdp == 2
+            and sections == 2
+            and seq & (seq - 1) == 0
+            and seq % fsdp == 0
+            and HEADS % seq == 0
+            and (HEADS // seq * HEAD) % 128 == 0
+            and rows % 16 == 0
+            and seq * rows <= 512
+            and (blocks[4].shape[1] // 2) % 16 == 0
+        )
+        if fits:
+            return fused_body(Plan(seq, fsdp, rows), *blocks)
+        return body(*blocks)
+
+    return run
+
+
 def solution(mesh):
     return jax.shard_map(
-        body,
+        pick(mesh),
         mesh=mesh,
         in_specs=(
             P("section", ("grp", "fsdp"), "seq", None),

time: 165 us -> 59.5 us (0.36)
  the two profiles are of different devices: /device:TPU:0 before, /device:TPU:25 now
where the time goes in v1:
time: 59.5 us; the launch traced here: 59.1 us
  Pallas kernels  48 us (81%)
  local copies, waits for them, and re-layouts  10.4 us (17%)
  between operations  0.66 us (1%)
    pallas_call x1, Pallas kernels, fused_body(): pl.pallas_call(functools.partial(fused, plan), out_shape=(jax.ShapeDtypeS...  48 us
    unnamed x16, local copies, waits for them, and re-layouts  10.4 us

profile of v1, /device:TPU:25, one launch (start us, length us, event | category | flops | bytes accessed | tf_op | source)
XLA Modules:
  0.0 59.1 jit_solution(3718347300400118282)
XLA Ops:
  0.6 0.9 %copy.11.hw = bf16[1,320,64]{2,1,0:T(8,128)(2,1)S(1)} copy(bf16[1,320,64]{1,2,0:T(8,128)(2,1)} %param.12) | data formatting | bytes 81920 | tf_op args[4]
  1.5 1.2 %copy.10.tw = bf16[1,256,960]{2,1,0:T(8,128)(2,1)S(1)} copy(bf16[1,256,960]{1,2,0:T(8,128)(2,1)} %param.11) | data formatting | bytes 983040 | tf_op args[3]
  2.8 0.0 copy-start
  2.8 2.9 %copy-done = bf16[1,1280,2560]{2,1,0:T(8,128)(2,1)S(1)} copy-done((bf16[1,1280,2560]{2,1,0:T(8,128)(2,1)S(1)}, bf16[1,1280,2560]{2,1,0:T(8,128)(2,1)}, u32[]{:S(2)}) %copy-start) | copy-done | bytes 6553624
  5.7 0.0 copy-start.1
  5.7 1.2 %copy-done.1 = bf16[1,1,64,7680]{3,2,1,0:T(8,128)(2,1)S(1)} copy-done((bf16[1,1,64,7680]{3,2,1,0:T(8,128)(2,1)S(1)}, bf16[1,1,64,7680]{3,2,1,0:T(8,128)(2,1)}, u32[]{:S(2)}) %copy-start.1) | copy-done | bytes 983064
  6.9 0.0 copy-start.2
  6.9 1.0 %copy-done.2 = bf16[1,1,64,2560]{3,2,1,0:T(8,128)(2,1)S(1)} copy-done((bf16[1,1,64,2560]{3,2,1,0:T(8,128)(2,1)S(1)}, bf16[1,1,64,2560]{3,2,1,0:T(8,128)(2,1)}, u32[]{:S(2)}) %copy-start.2) | copy-done | bytes 327704
  7.8 0.0 copy-start.3
  7.8 0.7 %copy-done.3 = f32[1,1,32,128]{3,2,1,0:T(8,128)S(1)} copy-done((f32[1,1,32,128]{3,2,1,0:T(8,128)S(1)}, f32[1,1,32,128]{3,2,1,0:T(8,128)}, u32[]{:S(2)}) %copy-start.3) | copy-done | bytes 16408
  8.5 0.0 copy-start.4
  8.5 0.7 %copy-done.4 = s32[1,1,2]{2,1,0:T(1,128)S(1)} copy-done((s32[1,1,2]{2,1,0:T(1,128)S(1)}, s32[1,1,2]{2,1,0:T(1,128)}, u32[]{:S(2)}) %copy-start.4) | copy-done | bytes 32
  9.2 0.0 copy-start.5
  9.2 0.7 %copy-done.5 = f32[1,128]{1,0:T(1,128)S(1)} copy-done((f32[1,128]{1,0:T(1,128)S(1)}, f32[1,128]{1,0:T(1,128)}, u32[]{:S(2)}) %copy-start.5) | copy-done | bytes 536
  9.9 48.0 %fused_step.1 = (f32[1,1,32,128]{3,2,1,0:T(8,128)S(1)}, f32[1,1,32,128]{3,2,1,0:T(8,128)S(1)}) custom-call(bf16[1,1,64,7680]{3,2,1,0:T(8,128)(2,1)S(1)} %copy-done.1, bf16[1,1,64,2560]{3,2,1,0:T(8,128)(2,1)S(1)} %copy-done.2, bf16[1,1280,2560]{2,1,0:T(8,128)(2,1)S(1)} %copy-done, bf16[1,256,960]{2,1,0:T(8,128)(2,1)S(1)} %copy.10.tw, ...), custom_call_target="tpu_custom_call" | custom-call | tf_op jit(solution)/shard_map/fused_step/pallas_call | solution.py:406
  57.9 0.6 %copy.14 = f32[1,1,32,128]{3,2,1,0:T(8,128)} copy(f32[1,1,32,128]{3,2,1,0:T(8,128)S(1)} %get-tuple-element.4) | data formatting | bytes 32768
  58.5 0.6 %copy.15 = f32[1,1,32,128]{3,2,1,0:T(8,128)} copy(f32[1,1,32,128]{3,2,1,0:T(8,128)S(1)} %get-tuple-element.5) | data formatting | bytes 32768
Async XLA Ops:
  2.8 2.9 %copy-start = (bf16[1,1280,2560]{2,1,0:T(8,128)(2,1)S(1)}, bf16[1,1280,2560]{2,1,0:T(8,128)(2,1)}, u32[]{:S(2)}) copy-start(bf16[1,1280,2560]{2,1,0:T(8,128)(2,1)} %ow.1) | copy-start | bytes 19660804
  5.7 1.2 %copy-start.1 = (bf16[1,1,64,7680]{3,2,1,0:T(8,128)(2,1)S(1)}, bf16[1,1,64,7680]{3,2,1,0:T(8,128)(2,1)}, u32[]{:S(2)}) copy-start(bf16[1,1,64,7680]{3,2,1,0:T(8,128)(2,1)} %qkv.1) | copy-start | bytes 2949124
  6.9 1.0 %copy-start.2 = (bf16[1,1,64,2560]{3,2,1,0:T(8,128)(2,1)S(1)}, bf16[1,1,64,2560]{3,2,1,0:T(8,128)(2,1)}, u32[]{:S(2)}) copy-start(bf16[1,1,64,2560]{3,2,1,0:T(8,128)(2,1)} %hid.1) | copy-start | bytes 983044
  7.8 0.7 %copy-start.3 = (f32[1,1,32,128]{3,2,1,0:T(8,128)S(1)}, f32[1,1,32,128]{3,2,1,0:T(8,128)}, u32[]{:S(2)}) copy-start(f32[1,1,32,128]{3,2,1,0:T(8,128)} %lat.1) | copy-start | bytes 49156
  8.5 0.7 %copy-start.4 = (s32[1,1,2]{2,1,0:T(1,128)S(1)}, s32[1,1,2]{2,1,0:T(1,128)}, u32[]{:S(2)}) copy-start(s32[1,1,2]{2,1,0:T(1,128)} %ts.1) | copy-start | bytes 28
  9.2 0.7 %copy-start.5 = (f32[1,128]{1,0:T(1,128)S(1)}, f32[1,128]{1,0:T(1,128)}, u32[]{:S(2)}) copy-start(f32[1,128]{1,0:T(1,128)} %constant.2.clone.freqs) | copy-start | bytes 1540

commit v2 on v1

--- a/solution.py
+++ b/solution.py
@@ -131,10 +131,10 @@
         self.group_in = self.heads * 3 * HEAD
         self.group_out = self.heads * HEAD
         per = max(1, self.heads // 4)
+        marks = sorted({*range(0, self.heads + 1, per), self.heads - 1, self.heads})
         self.chunks = []
         lo_in = lo_out = 0
-        for first in range(0, self.heads, per):
-            last = min(first + per, self.heads)
+        for first, last in zip(marks, marks[1:]):
             hi_in = min(up(last * 3 * HEAD, 128), self.group_in)
             hi_out = last * HEAD // 128 * 128 if last < self.heads else self.group_out
             self.chunks.append((first, last, (lo_in, hi_in), (lo_out, hi_out)))
@@ -145,7 +145,7 @@
 
 def fused(
     plan, qkv, hid, ow, tw, hw, lat, ts, freqs, vel_out, car_out,
-    qkv_v, ow_v, tw_v, hw_v, hid_v, lat_v, emb, mod_loc, mod_all, att, gath, own, part, got, packed, head_v,
+    qkv_v, ow_v, tw_v, hid_v, lat_v, emb, mod_loc, mod_all, att, gath, own, part, got, packed, head_v,
     upd, vel_v, step_v, step_in,
     loc_sem, own_sem, qs, qr, es, er, ms, mr, hxs, hxr, hzs, hzr, as_, ar, ps, pr, cs, cr,
 ):
@@ -170,7 +170,7 @@
     pl.semaphore_signal(barrier, inc=1, device_id={"section": 1 - s}, device_id_type=MESH)
 
     loads = [
-        pltpu.make_async_copy(hw.at[0], hw_v, loc_sem.at[0]),
+        pltpu.make_async_copy(hw.at[0], packed.at[slot], loc_sem.at[0]),
         pltpu.make_async_copy(tw.at[0], tw_v, loc_sem.at[1]),
         pltpu.make_async_copy(ow.at[0], ow_v, loc_sem.at[2]),
         pltpu.make_async_copy(hid.at[0, 0], hid_v, loc_sem.at[3]),
@@ -229,15 +229,13 @@
         in_copies.append(row)
 
     loads[0].wait()
-    half_rows = hw_v.shape[0] // 2
-    packed[slot] = jnp.concatenate([hw_v[:half_rows], hw_v[half_rows:]], axis=1)
     head_copy = remote(packed.at[slot], packed.at[slot], hxs, hxr, {"fsdp": other})
     head_copy.start()
 
     emb_copy.wait()
     loads[1].wait()
     both = emb[...].reshape(fsdp * 8, FREQ).astype(BF16)
-    mod = jnp.dot(both, tw_v[...], preferred_element_type=F32)
+    mod = lax.dot_general(both, tw_v[...], (((1,), (1,)), ((), ())), preferred_element_type=F32)
     for b in range(fsdp):
         mod_loc[b] = mod[b * 8 : b * 8 + 1]
     mod_all[slot] = mod_loc[f]
@@ -296,6 +294,51 @@
                         source, target, as_.at[c, d], ar.at[c, f, part_of_half], {"fsdp": half}
                     ).start()
 
+    def arrive(c):
+        lo, hi = plan.chunks[c][3]
+        for b in range(fsdp):
+            for i in range(per_half):
+                block = gath.at[b, i, :, lo:hi]
+                pltpu.make_async_copy(block, block, ar.at[c, b, i]).wait()
+
+    def tokens(i, lo, hi):
+        return gath[:, i, :, lo:hi].reshape(fsdp * rows, hi - lo)
+
+    def weights_of(i, lo, hi, cols):
+        return ow_v[i * plan.group_out + lo : i * plan.group_out + hi, cols]
+
+    loads[2].wait()
+    late = plan.chunks[-1][3][0]
+    for c in range(n_chunks - 1):
+        arrive(c)
+    blocks = [slice(k * plan.block, (k + 1) * plan.block) for k in range(plan.blocks)]
+    for cols in blocks:
+        total = jnp.zeros((fsdp * rows, plan.block), F32)
+        for i in range(per_half):
+            total += jnp.dot(
+                tokens(i, 0, late), weights_of(i, 0, late, cols), preferred_element_type=F32
+            )
+        for b in range(fsdp):
+            own[b, :, cols] = total[b * rows : (b + 1) * rows]
+    arrive(n_chunks - 1)
+    last_tokens = jnp.concatenate(
+        [tokens(i, late, plan.group_out) for i in range(per_half)], axis=1
+    )
+    part_copies = []
+    for k, cols in enumerate(blocks):
+        last_weights = jnp.concatenate(
+            [weights_of(i, late, plan.group_out, cols) for i in range(per_half)], axis=0
+        )
+        total = jnp.dot(last_tokens, last_weights, preferred_element_type=F32)
+        for b in range(fsdp):
+            projected = own[b, :, cols] + total[b * rows : (b + 1) * rows]
+            own[b, :, cols] = projected
+            part[b, :, cols] = projected.astype(BF16)
+        part_copies.append(
+            remote(part.at[other, :, cols], got.at[:, cols], ps.at[k], pr.at[k], {"fsdp": other})
+        )
+        part_copies[-1].start()
+
     head_copy.wait()
     head_copies = []
     for d in order:
@@ -305,40 +348,6 @@
             )
             head_copies[-1].start()
 
-    loads[2].wait()
-    for c, (_, _, _, (lo, hi)) in enumerate(plan.chunks):
-        for b in range(fsdp):
-            for i in range(per_half):
-                block = gath.at[b, i, :, lo:hi]
-                pltpu.make_async_copy(block, block, ar.at[c, b, i]).wait()
-    part_copies = []
-    for k in range(plan.blocks):
-        cols = slice(k * plan.block, (k + 1) * plan.block)
-        total = jnp.zeros((fsdp * rows, plan.block), F32)
-        for i in range(per_half):
-            total += jnp.dot(
-                gath[:, i].reshape(fsdp * rows, plan.group_out),
-                ow_v[i * plan.group_out : (i + 1) * plan.group_out, cols],
-                preferred_element_type=F32,
-            )
-        for b in range(fsdp):
-            own[b, :, cols] = total[b * rows : (b + 1) * rows]
-            part[b, :, cols] = total[b * rows : (b + 1) * rows].astype(BF16)
-        part_copies.append(
-            remote(part.at[other, :, cols], got.at[:, cols], ps.at[k], pr.at[k], {"fsdp": other})
-        )
-        part_copies[-1].start()
-
-    for copy in head_copies:
-        copy.wait_recv()
-    for j in range(seq * fsdp):
-        block = packed[j]
-        swapped = jnp.concatenate([block[:, PATCH:], block[:, :PATCH]], axis=1)
-        left = lax.broadcasted_iota(jnp.int32, block.shape, 1) < PATCH
-        head_v[2 * half_rows * j : 2 * half_rows * j + half_rows] = jnp.where(left, block, swapped)
-        head_v[2 * half_rows * j + half_rows : 2 * half_rows * (j + 1)] = jnp.where(
-            left, swapped, block
-        )
     for copy in mod_copies:
         copy.wait_recv()
     modulation = jnp.concatenate([mod_all[j] for j in range(seq * fsdp)], axis=1)
@@ -348,18 +357,29 @@
     loads[3].wait()
     loads[4].wait()
 
-    sums = jnp.zeros((rows, 1), F32)
-    for k in range(plan.blocks):
-        cols = slice(k * plan.block, (k + 1) * plan.block)
+    means, squares = [], []
+    for k, cols in enumerate(blocks):
         part_copies[k].wait_recv()
         projected = own[f, :, cols] + got[:, cols].astype(F32)
         now = hid_v[:, cols].astype(F32) + gate[:, cols] * projected
         upd[:, cols] = now
-        sums += jnp.sum(now, axis=-1, keepdims=True)
-    centred = upd[...] - sums * (1.0 / DIM)
-    variance = jnp.mean(centred * centred, axis=-1, keepdims=True)
-    normed = (centred * lax.rsqrt(variance + 1e-06) * (1.0 + scale) + shift).astype(BF16)
-    vel_v[...] = jnp.dot(normed, head_v[...], preferred_element_type=F32)
+        mean = jnp.mean(now, axis=-1, keepdims=True)
+        means.append(mean)
+        squares.append(jnp.sum((now - mean) * (now - mean), axis=-1, keepdims=True))
+    average = sum(means) * (1.0 / plan.blocks)
+    spread = sum((mean - average) * (mean - average) for mean in means) * plan.block
+    variance = (sum(squares) + spread) * (1.0 / DIM)
+    for copy in head_copies:
+        copy.wait_recv()
+    head_full = jnp.concatenate([packed[j] for j in range(seq * fsdp)], axis=1)
+    head_v[:PATCH] = head_full
+    head_v[PATCH:] = head_full
+    normed = (
+        (upd[...] - average) * lax.rsqrt(variance + 1e-06) * (1.0 + scale) + shift
+    ).astype(BF16)
+    vel_v[...] = lax.dot_general(
+        normed, head_v[...], (((1,), (1,)), ((), ())), preferred_element_type=F32
+    )
     even = vel_v[pl.ds(0, rows // 2, 2), :]
     odd = vel_v[pl.ds(1, rows // 2, 2), :]
     left = lax.broadcasted_iota(jnp.int32, even.shape, 1) < PATCH
@@ -395,13 +415,14 @@
 def fused_body(plan, head_inputs, hidden, out_weight, time_weight, head_weight, latent, timesteps):
     seq, fsdp, rows = plan.seq, plan.fsdp, plan.rows
     chunks = len(plan.chunks)
+    time_weight, head_weight = time_weight.swapaxes(1, 2), head_weight.swapaxes(1, 2)
     per_half = seq // fsdp
     half = FREQ // 2
     freqs = np.exp(-math.log(10000.0) * np.arange(half) / half).astype(np.float32)[None]
     dma = pltpu.SemaphoreType.DMA
     vmem = pltpu.VMEM
     whole = pl.BlockSpec(memory_space=pltpu.VMEM)
-    anywhere = pl.BlockSpec(memory_space=pl.ANY)
+    anywhere = pl.BlockSpec(memory_space=pltpu.HBM)
     parts = seq * fsdp
     return pl.pallas_call(
         functools.partial(fused, plan),
@@ -415,19 +436,18 @@
             vmem((seq * rows, plan.group_in), BF16),
             vmem(out_weight.shape[1:], BF16),
             vmem(time_weight.shape[1:], BF16),
-            vmem(head_weight.shape[1:], BF16),
             vmem((rows, DIM), BF16),
             vmem(latent.shape[2:], F32),
             vmem((fsdp, 8, FREQ), F32),
-            vmem((fsdp, 1, time_weight.shape[2]), F32),
-            vmem((parts, 1, time_weight.shape[2]), F32),
+            vmem((fsdp, 1, time_weight.shape[1]), F32),
+            vmem((parts, 1, time_weight.shape[1]), F32),
             vmem((seq * rows, plan.group_out), BF16),
             vmem((fsdp, per_half, rows, plan.group_out), BF16),
             vmem((fsdp, rows, DIM), F32),
             vmem((fsdp, rows, DIM), BF16),
             vmem((rows, DIM), BF16),
-            vmem((parts, head_weight.shape[1] // 2, 2 * PATCH), BF16),
-            vmem((DIM, 2 * PATCH), BF16),
+            vmem((parts, *head_weight.shape[1:]), BF16),
+            vmem((2 * PATCH, DIM), BF16),
             vmem((rows, DIM), F32),
             vmem((rows, 2 * PATCH), F32),
             vmem(latent.shape[2:], F32),
@@ -452,7 +472,7 @@
             dma,
         ],
         compiler_params=pltpu.CompilerParams(
-            collective_id=0, has_side_effects=True, vmem_limit_bytes=40 * 2**20
+            collective_id=0, has_side_effects=True, vmem_limit_bytes=58 * 2**20
         ),
         name="fused_step",
     )(head_inputs, hidden, out_weight, time_weight, head_weight, latent, timesteps, freqs)
@@ -473,7 +493,7 @@
             and (HEADS // seq * HEAD) % 128 == 0
             and rows % 16 == 0
             and seq * rows <= 512
-            and (blocks[4].shape[1] // 2) % 16 == 0
+            and DIM % 512 == 0
         )
         if fits:
             return fused_body(Plan(seq, fsdp, rows), *blocks)

time: 59.5 us -> 53.1 us (0.89)
  the two profiles are of different devices: /device:TPU:25 before, /device:TPU:0 now
where the time goes in v2:
time: 53.1 us; the launch traced here: 52.5 us
  Pallas kernels  49.2 us (93%)
  local copies, waits for them, and re-layouts  2.65 us (5%)
  between operations  0.64 us (1%)
    pallas_call x1, Pallas kernels, fused_body(): pl.pallas_call(functools.partial(fused, plan), out_shape=(jax.ShapeDtypeS...  49.2 us
    unnamed x2, local copies, waits for them, and re-layouts  2.65 us

profile of v2, /device:TPU:0, one launch (start us, length us, event | category | flops | bytes accessed | tf_op | source)
XLA Modules:
  0.0 52.5 jit_solution(7413498501119790349)
XLA Ops:
  0.6 49.2 %fused_step.1 = (f32[1,1,32,128]{3,2,1,0:T(8,128)}, f32[1,1,32,128]{3,2,1,0:T(8,128)}) custom-call(bf16[1,1,64,7680]{3,2,1,0:T(8,128)(2,1)} %qkv.1, bf16[1,1,64,2560]{3,2,1,0:T(8,128)(2,1)} %hid.1, bf16[1,1280,2560]{2,1,0:T(8,128)(2,1)} %ow.1, bf16[1,960,256]{2,1,0:T(8,128)(2,1)} %bitcast.2, bf16[1,64,320]{2,1,0:T(8,128)(2,1)} %bitcast.3, ...), custom_call_target="tpu_custom_call" | custom-call | tf_op jit(solution)/shard_map/fused_step/pallas_call | solution.py:427
  49.9 1.3 %copy.12 = f32[1,1,32,128]{3,2,1,0:T(8,128)} copy(f32[1,1,32,128]{3,2,1,0:T(8,128)} %get-tuple-element.4) | data formatting | bytes 32768
  51.2 1.3 %copy.13 = f32[1,1,32,128]{3,2,1,0:T(8,128)} copy(f32[1,1,32,128]{3,2,1,0:T(8,128)} %get-tuple-element.5) | data formatting | bytes 32768

commit v3 on v2

--- a/solution.py
+++ b/solution.py
@@ -144,13 +144,14 @@
 
 
 def fused(
-    plan, qkv, hid, ow, tw, hw, lat, ts, freqs, vel_out, car_out,
+    plan, qkv, hid, ow, tw, hw, lat, ts, freqs, out,
     qkv_v, ow_v, tw_v, hid_v, lat_v, emb, mod_loc, mod_all, att, gath, own, part, got, packed, head_v,
     upd, vel_v, step_v, step_in,
-    loc_sem, own_sem, qs, qr, es, er, ms, mr, hxs, hxr, hzs, hzr, as_, ar, ps, pr, cs, cr,
+    loc_sem, own_sem, qs, qr, es, er, ms, mr, hxs, hxr, hzs, hzr, gs, gr, as_, ar, ps, pr, cs, cr,
 ):
     seq, fsdp, rows = plan.seq, plan.fsdp, plan.rows
     z, f, s = lax.axis_index("seq"), lax.axis_index("fsdp"), lax.axis_index("section")
+    g = lax.axis_index("grp")
     other = 1 - f
     slot = z * fsdp + f
     per_half = seq // fsdp
@@ -168,6 +169,7 @@
                 to = {"seq": z ^ dz, "fsdp": f ^ df}
                 pl.semaphore_signal(barrier, inc=1, device_id=to, device_id_type=MESH)
     pl.semaphore_signal(barrier, inc=1, device_id={"section": 1 - s}, device_id_type=MESH)
+    pl.semaphore_signal(barrier, inc=1, device_id={"grp": 1 - g}, device_id_type=MESH)
 
     loads = [
         pltpu.make_async_copy(hw.at[0], packed.at[slot], loc_sem.at[0]),
@@ -200,17 +202,10 @@
     for load in loads:
         load.start()
 
-    t_now = ts[0, 0, 0].astype(F32)
-    angle = t_now * jnp.broadcast_to(freqs[...], (8, FREQ // 2))
-    emb[f, :, : FREQ // 2] = jnp.cos(angle)
-    emb[f, :, FREQ // 2 :] = jnp.sin(angle)
-
-    pl.semaphore_wait(barrier, seq * fsdp)
+    pl.semaphore_wait(barrier, seq * fsdp + 1)
 
     order = sorted(range(1, seq), reverse=True)
     sends = []
-    emb_copy = remote(emb.at[f], emb.at[f], es, er, {"fsdp": other})
-    emb_copy.start()
     in_copies = []
     for c, (_, _, span, _) in enumerate(plan.chunks):
         row = []
@@ -227,6 +222,14 @@
             )
             row[-1].start()
         in_copies.append(row)
+
+    t_now = ts[0, 0, 0].astype(F32)
+    angle = t_now * jnp.broadcast_to(freqs[...], (8, FREQ // 2))
+    emb[f, :, : FREQ // 2] = jnp.cos(angle)
+    emb[f, :, FREQ // 2 :] = jnp.sin(angle)
+
+    emb_copy = remote(emb.at[f], emb.at[f], es, er, {"fsdp": other})
+    emb_copy.start()
 
     loads[0].wait()
     head_copy = remote(packed.at[slot], packed.at[slot], hxs, hxr, {"fsdp": other})
@@ -321,6 +324,20 @@
         for b in range(fsdp):
             own[b, :, cols] = total[b * rows : (b + 1) * rows]
     arrive(n_chunks - 1)
+    head_copy.wait()
+    head_copies = []
+    half_rows = PATCH // 2
+    my_half = pl.ds(pl.multiple_of(g * half_rows, half_rows), half_rows)
+    for d in order:
+        for b, column in enumerate((f, other)):
+            source = packed.at[z * fsdp + column, my_half]
+            head_copies.append(
+                (
+                    remote(source, source, hzs.at[b, d], hzr.at[b, d], {"seq": z ^ d}),
+                    (z ^ d) * fsdp + column,
+                )
+            )
+            head_copies[-1][0].start()
     last_tokens = jnp.concatenate(
         [tokens(i, late, plan.group_out) for i in range(per_half)], axis=1
     )
@@ -339,14 +356,14 @@
         )
         part_copies[-1].start()
 
-    head_copy.wait()
-    head_copies = []
-    for d in order:
-        for b, index in enumerate((slot, z * fsdp + other)):
-            head_copies.append(
-                remote(packed.at[index], packed.at[index], hzs.at[b, d], hzr.at[b, d], {"seq": z ^ d})
-            )
-            head_copies[-1].start()
+    pass_copies = []
+    for copy, index in head_copies:
+        copy.wait_recv()
+        source = packed.at[index, my_half]
+        pass_copies.append(
+            remote(source, source, gs.at[len(pass_copies)], gr.at[len(pass_copies)], {"grp": 1 - g})
+        )
+        pass_copies[-1].start()
 
     for copy in mod_copies:
         copy.wait_recv()
@@ -369,7 +386,7 @@
     average = sum(means) * (1.0 / plan.blocks)
     spread = sum((mean - average) * (mean - average) for mean in means) * plan.block
     variance = (sum(squares) + spread) * (1.0 / DIM)
-    for copy in head_copies:
+    for copy in pass_copies:
         copy.wait_recv()
     head_full = jnp.concatenate([packed[j] for j in range(seq * fsdp)], axis=1)
     head_v[:PATCH] = head_full
@@ -384,7 +401,7 @@
     odd = vel_v[pl.ds(1, rows // 2, 2), :]
     left = lax.broadcasted_iota(jnp.int32, even.shape, 1) < PATCH
     velocity = jnp.where(left, even, odd)
-    vel_out[0, 0] = velocity
+    out[0] = velocity
 
     unit = jnp.full((1, 2 * PATCH), ts[0, 0, 0].astype(F32), F32) / 1000.0
     unit_next = jnp.full((1, 2 * PATCH), ts[0, 0, 1].astype(F32), F32) / 1000.0
@@ -396,7 +413,7 @@
     for row in in_copies:
         for copy in row:
             copy.wait_send()
-    for copy in mod_copies + head_copies + part_copies:
+    for copy in mod_copies + [copy for copy, _ in head_copies] + pass_copies + part_copies:
         copy.wait_send()
     for c, (_, _, _, (lo, hi)) in enumerate(plan.chunks):
         for d in order:
@@ -409,7 +426,7 @@
             pltpu.make_async_copy(block, block, as_.at[c, 0]).wait()
 
     swap.wait()
-    car_out[0, 0] = step_in[...]
+    out[1] = step_in[...]
 
 
 def fused_body(plan, head_inputs, hidden, out_weight, time_weight, head_weight, latent, timesteps):
@@ -424,14 +441,11 @@
     whole = pl.BlockSpec(memory_space=pltpu.VMEM)
     anywhere = pl.BlockSpec(memory_space=pltpu.HBM)
     parts = seq * fsdp
-    return pl.pallas_call(
+    out = pl.pallas_call(
         functools.partial(fused, plan),
-        out_shape=(
-            jax.ShapeDtypeStruct(latent.shape, F32),
-            jax.ShapeDtypeStruct(latent.shape, F32),
-        ),
+        out_shape=jax.ShapeDtypeStruct((2, *latent.shape[2:]), F32),
         in_specs=[anywhere] * 6 + [pl.BlockSpec(memory_space=pltpu.SMEM), whole],
-        out_specs=(whole, whole),
+        out_specs=whole,
         scratch_shapes=[
             vmem((seq * rows, plan.group_in), BF16),
             vmem(out_weight.shape[1:], BF16),
@@ -464,6 +478,8 @@
             dma,
             dma((fsdp, seq)),
             dma((fsdp, seq)),
+            dma((fsdp * (seq - 1),)),
+            dma((fsdp * (seq - 1),)),
             dma((chunks, seq)),
             dma((chunks, fsdp, per_half)),
             dma((plan.blocks,)),
@@ -476,10 +492,12 @@
         ),
         name="fused_step",
     )(head_inputs, hidden, out_weight, time_weight, head_weight, latent, timesteps, freqs)
+    return out[0].reshape(latent.shape), out[1].reshape(latent.shape)
 
 
 def pick(mesh):
     seq, fsdp, sections = mesh.shape["seq"], mesh.shape["fsdp"], mesh.shape["section"]
+    groups = mesh.shape["grp"]
 
     def run(*blocks):
         samples, rows = blocks[0].shape[1:3]
@@ -487,6 +505,7 @@
             samples == 1
             and fsdp == 2
             and sections == 2
+            and groups == 2
             and seq & (seq - 1) == 0
             and seq % fsdp == 0
             and HEADS % seq == 0

time: 53.1 us -> 50.7 us (0.955)
  local copies, waits for them, and re-layouts: 2.65 us -> 1.35 us
  Pallas kernels: 49.2 us -> 48.4 us
    unnamed x2 -> x0, local copies, waits for them, and re-layouts: 2.65 us -> none
    another operation x0 -> x1, local copies, waits for them, and re-layouts: none -> 1.35 us  [fused_body(): return (out[0].reshape(latent.shape), out[1].reshape(latent.shape))]
    pallas_call x1, Pallas kernels: 49.2 us -> 48.4 us  [fused_body(): pl.pallas_call(functools.partial(fused, plan), out_shape=jax.ShapeDtypeSt...]
where the time goes in v3:
time: 50.7 us; the launch traced here: 50.4 us
  Pallas kernels  48.4 us (95%)
  local copies, waits for them, and re-layouts  1.35 us (3%)
  between operations  0.64 us (1%)
    pallas_call x1, Pallas kernels, fused_body(): pl.pallas_call(functools.partial(fused, plan), out_shape=jax.ShapeDtypeSt...  48.4 us
    another operation x1, local copies, waits for them, and re-layouts, fused_body(): return (out[0].reshape(latent.shape), out[1].reshape(latent.shape))  1.35 us

profile of v3, /device:TPU:0, one launch (start us, length us, event | category | flops | bytes accessed | tf_op | source)
XLA Modules:
  0.0 50.4 jit_solution(3285376911559758554)
XLA Ops:
  0.6 48.4 %fused_step.1 = f32[2,32,128]{2,1,0:T(8,128)} custom-call(bf16[1,1,64,7680]{3,2,1,0:T(8,128)(2,1)} %qkv.1, bf16[1,1,64,2560]{3,2,1,0:T(8,128)(2,1)} %hid.1, bf16[1,1280,2560]{2,1,0:T(8,128)(2,1)} %ow.1, bf16[1,960,256]{2,1,0:T(8,128)(2,1)} %bitcast.6, bf16[1,64,320]{2,1,0:T(8,128)(2,1)} %bitcast.7, f32[1,1,32,128]{3,2,1,0:T(8,128)} %lat.1, s32[1,1,2]{2,1,0:T(1,128)} %ts.1, ...), custom_call_target="tpu_custom_call" | custom-call | tf_op jit(solution)/shard_map/fused_step/pallas_call | solution.py:444
  49.1 1.3 %slice_bitcast_fusion = (f32[1,1,32,128]{3,2,1,0:T(8,128)}, f32[1,1,32,128]{3,2,1,0:T(8,128)}) fusion(f32[2,32,128]{2,1,0:T(8,128)} %fused_step.1), kind=kLoop, calls=%fused_computation | loop fusion | bytes 65536 | tf_op jit(solution)/shard_map/reshape;squeeze | solution.py:495
